TPU v7x, 512 devices: a whole 4x4x16 slice. The times are simulated.
512 devices in a mesh: dp: 16 (over z), expert: 8 (over y_lo, x), tensor: 4 (over y_hi, core).
Axes of the slice: x: 4, y: 4 (y_hi: 2, y_lo: 2; y = y_hi * 2 + y_lo), z: 16, core: 2. Of those that a mesh axis runs over, the one named last changes fastest.
Arguments:
- tokens: bfloat16 [16, 2, 352, 2048], P('dp'), may hold values from -6 to 6
- upstream: bfloat16 [16, 2, 352, 7168], P('dp', None, None, ('expert', 'tensor')), may hold values from -2 to 2
- router: float32 [16, 2, 8], replicated, may hold values from 0.05 to 1
- counts: int32 [16], replicated, may hold values from 0 to 2, as said below
- w_gate: bfloat16 [8, 2048, 8, 896], P('expert', 'dp', None, 'tensor'), may hold values from -0.125 to 0.125
- w_up: bfloat16 [8, 2048, 8, 896], P('expert', 'dp', None, 'tensor'), may hold values from -0.125 to 0.125
Outputs:
- tokens_grad: bfloat16 [16, 2, 352, 2048], P('dp', None, ('expert', 'tensor'))
- gate_grad: bfloat16 [8, 2048, 8, 896], P('expert', 'dp', None, 'tensor')
- up_grad: bfloat16 [8, 2048, 8, 896], P('expert', 'dp', None, 'tensor')
Inputs may be any that keep to these rules, and one draw needn't show every extreme that they name: The counts sum to 16; one or more groups hold 2 segments, and as many groups hold none.
All inputs are finite; a program needn't handle non-finite values.
Results may differ from a plain program's by a relative error of at most 0.02.
Values may be sent and summed in bfloat16 or wider, within the bound.
A program may use at most 64 MiB of HBM per device.

v0:
```python
import functools

import jax
import jax.numpy as jnp
from jax import lax
from jax.experimental import pallas as pl
from jax.experimental.pallas import tpu as pltpu
from jax.sharding import Mesh, PartitionSpec as P

MESH = pl.DeviceIdType.MESH
PLANE = ("y_lo", "x", "y_hi")
EXPERT = ("y_lo", "x")
PIECES = ((0, 48), (48, 48), (96, 48), (144, 32))
PARTS = ((0, 256), (256, 256), (512, 256), (768, 128))
NT = (((1,), (1,)), ((), ()))
TN = (((0,), (0,)), ((), ()))


def ring_kernel(
    n, rv, wx, tok, ups, tg, wg, merged, stage, contrib, inbox, spread, acc,
    rs_send, rs_recv, ag_send, ag_recv,
):
    z = lax.axis_index("dp")
    half = n // 2
    experts = wx.shape[0]
    right, left = lax.rem(z + 1, n), lax.rem(z + n - 1, n)
    towards = (right, left)

    def ahead(way, d):
        return lax.rem(z + d, n) if way == 0 else lax.rem(z + n - d, n)

    def behind(way, d):
        return ahead(1 - way, d)

    barrier = pltpu.get_barrier_semaphore()
    for other in towards:
        pl.semaphore_signal(barrier, inc=1, device_id={"dp": other}, device_id_type=MESH)
    pl.semaphore_wait(barrier, 2)

    def rs_copy(way, d, p, src):
        rows = pl.ds(*PIECES[p])
        return pltpu.make_async_remote_copy(
            src_ref=src.at[rows],
            dst_ref=inbox.at[way, d - 1, rows],
            send_sem=rs_send.at[way, d - 1, p],
            recv_sem=rs_recv.at[way, d - 1, p],
            device_id={"dp": towards[way]},
            device_id_type=MESH,
        )

    def ag_copy(way, d, p, v):
        rows = pl.ds(*PIECES[p])
        return pltpu.make_async_remote_copy(
            src_ref=spread.at[v, rows],
            dst_ref=spread.at[v, rows],
            send_sem=ag_send.at[way, d - 1, p],
            recv_sem=ag_recv.at[way, d - 1, p],
            device_id={"dp": towards[way]},
            device_id_type=MESH,
        )

    def merge(v):
        weights = [rv[v, e] for e in range(experts)]

        def block(i, carry):
            rows = pl.ds(pl.multiple_of(i * 64, 64), 64)
            total = weights[0] * wx[0, rows].astype(jnp.float32)
            for e in range(1, experts):
                total = total + weights[e] * wx[e, rows].astype(jnp.float32)
            merged[v, rows] = total.astype(jnp.bfloat16)
            return carry

        lax.fori_loop(0, wx.shape[1] // 64, block, 0)

    def partial(v):
        return lax.dot_general(tok[v], merged[v], NT, preferred_element_type=jnp.float32)

    def start_pieces(d, way):
        longer = (0, 1) if way == 0 else (2, 3)
        return longer if d == half else tuple(p for p in range(4) if p not in longer)

    far = ahead(0, half)
    merge(far)
    stage[0] = partial(far).astype(jnp.bfloat16)
    for way in (0, 1):
        for p in start_pieces(half, way):
            rs_copy(way, half, p, stage.at[0]).start()
    for way in (0, 1):
        v = ahead(way, half - 1)
        merge(v)
        contrib[(half - 1) % 2, way] = partial(v)
        for p in start_pieces(half - 1, way):
            rows = pl.ds(*PIECES[p])
            stage[1, rows] = contrib[(half - 1) % 2, way, rows].astype(jnp.bfloat16)
            rs_copy(way, half - 1, p, stage.at[1]).start()

    def pass_on(way, d, p):
        rows = pl.ds(*PIECES[p])
        rs_copy(way, d + 1, p, inbox.at[way, d]).wait_recv()
        total = inbox[way, d, rows].astype(jnp.float32) + contrib[lax.rem(d, 2), way, rows]
        inbox[way, d, rows] = total.astype(jnp.bfloat16)
        rs_copy(way, d, p, inbox.at[way, d]).start()

    def prepare(d, i):
        way, second = i // 2, i % 2
        v = ahead(way, d)
        if second:
            contrib[lax.rem(d, 2), way] = partial(v)
        else:
            merge(v)

    for i in range(4):
        if i < 2:
            pass_on(0, half - 1, start_pieces(half, 0)[i])
            pass_on(1, half - 1, start_pieces(half, 1)[i])
        prepare(half - 2, i)

    def rs_step(i, carry):
        d = half - 2 - i
        for i, (up, down) in enumerate(((2, 0), (3, 1), (0, 2), (1, 3))):
            pass_on(0, d, up)
            pass_on(1, d, down)
            prepare(d - 1, i)
        return carry

    lax.fori_loop(0, half - 2, rs_step, 0)

    def gate_part(gate, up, flowing):
        s = jax.nn.sigmoid(gate)
        return (flowing * up * s * (1.0 + gate * (1.0 - s))).astype(jnp.bfloat16)

    def up_part(gate, flowing):
        return (flowing * gate * jax.nn.sigmoid(gate)).astype(jnp.bfloat16)

    for p in range(4):
        rows = pl.ds(*PIECES[p])
        for way in (0, 1):
            rs_copy(way, 1, p, inbox.at[way, 0]).wait_recv()
        pre = (
            inbox[0, 0, rows].astype(jnp.float32)
            + inbox[1, 0, rows].astype(jnp.float32)
            + contrib[0, 0, rows]
        )
        flowing = ups[rows].astype(jnp.float32)
        gate, mixed, up = pre[:, :384], pre[:, 384:512], pre[:, 512:]
        spread[z, rows, :384] = gate_part(gate, up, flowing[:, :384])
        spread[z, rows, 512:] = up_part(gate, flowing[:, :384])
        low = lax.broadcasted_iota(jnp.int32, mixed.shape, 1) < 64
        rolled = pltpu.roll(mixed, 64, 1)
        gate, up = jnp.where(low, mixed, rolled), jnp.where(low, rolled, mixed)
        spread[z, rows, 384:512] = jnp.where(
            low, gate_part(gate, up, flowing[:, 384:]), up_part(gate, flowing[:, 384:])
        )
        for way in (0, 1):
            ag_copy(way, 1, p, z).start()

    acc[...] = jnp.zeros_like(acc)

    def back(owners, i):
        rows, hidden = pl.ds(*PIECES[i]), pl.ds(*PARTS[i])
        terms = []
        for v in owners:
            tg[v, rows] = jnp.dot(
                spread[v, rows], merged[v], preferred_element_type=jnp.float32
            ).astype(jnp.bfloat16)
            terms.append(
                lax.dot_general(
                    spread[v, :, hidden], tok[v], TN, preferred_element_type=jnp.float32
                )
            )
        for e in range(experts):
            total = acc[e, hidden]
            for v, term in zip(owners, terms):
                total = total + rv[v, e] * term
            acc[e, hidden] = total

    def receive(way, d, p):
        ag_copy(way, d, p, behind(way, d)).wait_recv()

    def forward(way, d, p):
        ag_copy(way, d + 1, p, behind(way, d)).start()

    def ag_step(d, owners, last):
        for p in range(4):
            for way in (0, 1):
                receive(way, d, p)
                if not last or p in start_pieces(half, way):
                    forward(way, d, p)
            back(owners, p)

    ag_step(1, (z,), False)
    lax.fori_loop(
        2,
        half - 1,
        lambda d, carry: (ag_step(d, (behind(0, d - 1), behind(1, d - 1)), False), carry)[1],
        0,
    )
    ag_step(half - 1, (behind(0, half - 2), behind(1, half - 2)), True)
    for i in range(4):
        back((behind(0, half - 1), behind(1, half - 1)), i)
    for way in (0, 1):
        for p in start_pieces(half, way):
            receive(way, half, p)
    for i in range(4):
        back((far,), i)
    wg[...] = acc[...].astype(jnp.bfloat16)

    for way in (0, 1):
        for p in range(4):
            reach = half if p in start_pieces(half, way) else half - 1

            def sent(d, carry, way=way, p=p):
                rs_copy(way, d, p, inbox.at[way, 0]).wait_send()
                ag_copy(way, d, p, 0).wait_send()
                return carry

            lax.fori_loop(1, reach + 1, sent, 0)


def ring(n, rv, wx, tok, ups):
    experts, hidden, depth = wx.shape
    rows = tok.shape[1]
    half = n // 2
    vmem = pl.BlockSpec(memory_space=pltpu.VMEM)
    return pl.pallas_call(
        functools.partial(ring_kernel, n),
        out_shape=(
            jax.ShapeDtypeStruct((n, rows, depth), jnp.bfloat16),
            jax.ShapeDtypeStruct((experts, hidden, depth), jnp.bfloat16),
        ),
        in_specs=[pl.BlockSpec(memory_space=pltpu.SMEM), vmem, vmem, vmem],
        out_specs=(vmem, vmem),
        scratch_shapes=[
            pltpu.VMEM((n, hidden, depth), jnp.bfloat16),
            pltpu.VMEM((2, rows, hidden), jnp.bfloat16),
            pltpu.VMEM((2, 2, rows, hidden), jnp.float32),
            pltpu.VMEM((2, half, rows, hidden), jnp.bfloat16),
            pltpu.VMEM((n, rows, hidden), jnp.bfloat16),
            pltpu.VMEM((experts, hidden, depth), jnp.float32),
            pltpu.SemaphoreType.DMA((2, half, 4)),
            pltpu.SemaphoreType.DMA((2, half, 4)),
            pltpu.SemaphoreType.DMA((2, half, 4)),
            pltpu.SemaphoreType.DMA((2, half, 4)),
        ],
        compiler_params=pltpu.CompilerParams(
            collective_id=0, has_side_effects=True, vmem_limit_bytes=48 * 2**20
        ),
    )(rv, wx, tok, ups)


def swap(a):
    return lax.ppermute(a, "core", [(0, 1), (1, 0)])


def exchange(a, axes):
    return lax.all_to_all(a, axes, split_axis=0, concat_axis=0, tiled=True)


def local(tokens, upstream, router, counts, w_gate, w_up):
    n = lax.axis_size("dp")
    z = lax.axis_index("dp")
    core = lax.axis_index("core")
    place = lax.axis_index(PLANE)
    _, slots, seg_len, width = tokens.shape
    _, depth, blocks, cols = w_gate.shape
    plane = lax.axis_size(PLANE)
    lines = seg_len // (2 * plane)
    first = core == 0

    empty, double = counts == 0, counts == 2
    before = jnp.tril(jnp.ones((n, n), jnp.int32), -1)
    empty_rank = jnp.sum(before * empty[None, :].astype(jnp.int32), 1)
    double_rank = jnp.sum(before * double[None, :].astype(jnp.int32), 1)
    pairs = (empty[:, None] & double[None, :]) & (empty_rank[:, None] == double_rank[None, :])
    ids = jnp.arange(n, dtype=jnp.int32)
    partner = jnp.sum(jnp.where(pairs, ids[None, :], 0), 1)
    helper = jnp.sum(jnp.where(pairs, ids[:, None], 0), 0)
    helped = jnp.sum(pairs.astype(jnp.int32), 0) > 0
    lent = jnp.sum(jnp.where(pairs[:, :, None], router[None, :, 1, :], 0.0), 1)
    rv = jnp.where(empty[:, None], lent, router[:, 0, :])

    own = jnp.concatenate([w_gate[0].transpose(1, 2, 0), w_up[0].transpose(1, 2, 0)], 1)
    own = exchange(own, EXPERT)
    other = swap(own)
    lo, hi = jnp.where(first, own, other), jnp.where(first, other, own)
    cut = 64
    wx = jnp.concatenate(
        [
            lo[:, :cols],
            hi[:, :cols],
            hi[:, 2 * cols - cut :],
            lo[:, cols:],
            hi[:, cols : 2 * cols - cut],
        ],
        1,
    )

    mine = lax.dynamic_slice_in_dim(tokens[0], (place * 2 + core) * lines, lines, 1)
    mine = exchange(mine.reshape(slots, lines, n, width // n).transpose(2, 0, 1, 3), "dp")
    mine = jnp.where(empty[:, None, None], jnp.take(mine[:, 1], partner, 0), mine[:, 0])
    tok = lax.all_gather(mine, PLANE).transpose(1, 0, 2, 3).reshape(n, plane * lines, -1)

    up = upstream[0].reshape(slots, plane, 2, lines, cols)
    own_up = jnp.where(first, up[:, :, 0], up[:, :, 1])
    other_up = swap(jnp.where(first, up[:, :, 1], up[:, :, 0]))
    up = jnp.concatenate(
        [jnp.where(first, own_up, other_up), jnp.where(first, other_up, own_up)], -1
    )
    moved = exchange(up[1], "dp")
    moved = exchange(jnp.take(moved, partner, 0), "dp")
    ups = jnp.where(counts[z] == 0, moved, up[0]).reshape(plane * lines, 2 * cols)
    ups = jnp.concatenate([ups, ups[:, 2 * cols - cut :]], 1)

    tg, wg = ring(n, rv, wx, tok, ups)

    tg = tg.reshape(n, plane, lines, -1).transpose(1, 0, 2, 3)
    tg = jnp.sum(exchange(tg, PLANE).reshape(plane, n, lines, -1).astype(jnp.float32), 0)
    tg = tg.astype(jnp.bfloat16)
    slot0 = jnp.where(empty[:, None, None], 0, tg)
    slot1 = jnp.where(helped[:, None, None], jnp.take(tg, helper, 0), 0)
    tg = exchange(jnp.stack([slot0, slot1], 1), "dp")
    tokens_grad = tg.transpose(1, 2, 0, 3).reshape(1, slots, lines, width)

    lo = jnp.concatenate([wg[:, :cols], wg[:, 2 * cols + cut : 3 * cols + cut]], 1)
    hi = jnp.concatenate(
        [wg[:, cols : 2 * cols], wg[:, 3 * cols + cut :], wg[:, 2 * cols : 2 * cols + cut]], 1
    )
    got = swap(jnp.where(first, hi, lo)).astype(jnp.float32)
    total = (jnp.where(first, lo, hi).astype(jnp.float32) + got).astype(jnp.bfloat16)
    total = exchange(total, EXPERT)
    gate_grad = total[:, :cols].transpose(2, 0, 1)[None]
    up_grad = total[:, cols:].transpose(2, 0, 1)[None]
    return (tokens_grad, gate_grad, up_grad)


def solution(mesh):
    shape = (mesh.shape["dp"], 2, mesh.shape["expert"] // 2, mesh.shape["tensor"] // 2, 2)
    fine = Mesh(mesh.devices.reshape(shape), ("dp", "y_lo", "x", "y_hi", "core"))
    tensor = ("y_hi", "core")
    weights = P(EXPERT, "dp", None, tensor)
    in_specs = (
        P("dp", None, None, None),
        P("dp", None, None, EXPERT + tensor),
        P(),
        P(),
        weights,
        weights,
    )
    out_specs = (P("dp", None, EXPERT + tensor, None), weights, weights)
    return jax.shard_map(local, mesh=fine, in_specs=in_specs, out_specs=out_specs, check_vma=False)
```

profile of v0, /device:TPU:2, one launch (start us, length us, event | category | flops | bytes accessed | tf_op | source)
XLA Modules:
  0.0 311.3 jit_solution(7986874980030781176)
XLA Ops:
  0.7 1.8 copy-done
  3.3 15.2 %all-to-all-start.1 = ((bf16[16,2,11,128]{3,1,2,0:T(2,128)(2,1)}), bf16[16,2,11,128]{3,1,2,0:T(2,128)(2,1)S(1)}, u32[]{:S(2)}, u32[]{:S(2)}) async-start(bf16[16,2,11,128]{3,1,2,0:T(2,128)(2,1)} %copy.84), calls=%async_computation.1 | async-start | bytes 180224 | tf_op jit(solution)/shard_map/all_to_all | solution.py:256
  20.1 1.9 collective-permute-start.1
  25.8 6.0 %all-to-all-done.1 = bf16[16,2,11,128]{3,1,2,0:T(2,128)(2,1)S(1)} async-done(((bf16[16,2,11,128]{3,1,2,0:T(2,128)(2,1)}), bf16[16,2,11,128]{3,1,2,0:T(2,128)(2,1)S(1)}, u32[]{:S(2)}, u32[]{:S(2)}) %all-to-all-start.1) | async-done | bytes 90144 | tf_op jit(solution)/shard_map/all_to_all | solution.py:256
  32.5 6.0 %all-to-all-start.2 = ((bf16[16,11,448]{2,1,0:T(8,128)(2,1)}), bf16[16,11,448]{2,1,0:T(8,128)(2,1)S(1)}, u32[]{:S(2)}, u32[]{:S(2)}) async-start(bf16[16,11,448]{2,1,0:T(8,128)(2,1)} %bitcast.87), calls=%async_computation.2 | async-start | bytes 524288 | tf_op jit(solution)/shard_map/all_to_all | solution.py:256
  38.5 2.2 pad_maximum_fusion
  41.2 15.8 %all-to-all-done.2 = bf16[16,11,448]{2,1,0:T(8,128)(2,1)S(1)} async-done(((bf16[16,11,448]{2,1,0:T(8,128)(2,1)}), bf16[16,11,448]{2,1,0:T(8,128)(2,1)S(1)}, u32[]{:S(2)}, u32[]{:S(2)}) %all-to-all-start.2) | async-done | bytes 157728 | tf_op jit(solution)/shard_map/all_to_all | solution.py:256
  57.0 5.8 %all-to-all-start = ((bf16[8,448,128]{2,1,0:T(8,128)(2,1)}), bf16[8,448,128]{2,1,0:T(8,128)(2,1)}, u32[]{:S(2)}, u32[]{:S(2)}) async-start(bf16[8,448,128]{2,1,0:T(8,128)(2,1)} %pad_maximum_fusion), calls=%async_computation | async-start | bytes 1835008 | tf_op jit(solution)/shard_map/all_to_all | solution.py:256
  66.7 5.9 %all-to-all-done = bf16[8,448,128]{2,1,0:T(8,128)(2,1)} async-done(((bf16[8,448,128]{2,1,0:T(8,128)(2,1)}), bf16[8,448,128]{2,1,0:T(8,128)(2,1)}, u32[]{:S(2)}, u32[]{:S(2)}) %all-to-all-start) | async-done | bytes 917536 | tf_op jit(solution)/shard_map/all_to_all | solution.py:256
  72.6 9.5 %all-to-all-start.3 = ((bf16[16,11,448]{2,1,0:T(8,128)(2,1)}), bf16[16,11,448]{2,1,0:T(8,128)(2,1)S(1)}, u32[]{:S(2)}, u32[]{:S(2)}) async-start(bf16[16,11,448]{2,1,0:T(8,128)(2,1)} %broadcast_select_fusion.6), calls=%async_computation.3 | async-start | bytes 524288 | tf_op jit(solution)/shard_map/all_to_all | solution.py:256
  84.5 2.0 gather_fusion.1
  86.5 1.9 collective-permute-start
  89.5 40.7 %all-gather = bf16[256,11,128]{2,0,1:T(8,128)(2,1)S(1)} all-gather(bf16[16,11,128]{2,0,1:T(8,128)(2,1)S(1)} %copy.87), channel_id=2, replica_groups=mesh['dp'=16,'y_lo'=2,'x'=4,'y_hi'=2,'core'=2] {'y_lo','x','y_hi'}, dimensions={0}, use_global_device_ids=true | all-gather | bytes 765952 | tf_op jit(solution)/shard_map/all_gather | solution.py:301
  135.1 110.2 %shard_map.85 = (bf16[16,176,128]{2,1,0:T(8,128)(2,1)S(1)}, bf16[8,896,128]{2,1,0:T(8,128)(2,1)S(1)}) custom-call(f32[16,8]{1,0:T(8,128)S(1)} %broadcast_select_fusion.7.rv, bf16[8,896,128]{2,1,0:T(8,128)(2,1)S(1)} %slice_dynamic-update-slice_fusion.3.wx, bf16[16,176,128]{2,1,0:T(8,128)(2,1)S(1)} %copy-done.1, bf16[176,512]{1,0:T(8,128)(2,1)S(1)} %pad_maximum_fusion.4.ups), custom_call_target="tpu_custom_call" | custom-call | tf_op jit(solution)/shard_map/pallas_call | solution.py:225
  248.4 6.4 %all-to-all-start.4 = ((bf16[16,16,11,128]{3,1,2,0:T(8,128)(2,1)}), bf16[16,16,11,128]{3,1,2,0:T(8,128)(2,1)}, u32[]{:S(2)}, u32[]{:S(2)}) async-start(bf16[16,16,11,128]{3,1,2,0:T(8,128)(2,1)} %bitcast.84), calls=%async_computation.4 | async-start | bytes 1441792 | tf_op jit(solution)/shard_map/all_to_all | solution.py:256
  258.3 1.9 collective-permute-start.2
  260.2 4.4 %all-to-all-done.4 = bf16[16,16,11,128]{3,1,2,0:T(8,128)(2,1)} async-done(((bf16[16,16,11,128]{3,1,2,0:T(8,128)(2,1)}), bf16[16,16,11,128]{3,1,2,0:T(8,128)(2,1)}, u32[]{:S(2)}, u32[]{:S(2)}) %all-to-all-start.4) | async-done | bytes 720928 | tf_op jit(solution)/shard_map/all_to_all | solution.py:256
  266.5 2.0 gather_fusion.2
  270.3 10.4 %all-to-all-start.5 = ((bf16[16,2,11,128]{3,1,2,0:T(2,128)(2,1)}), bf16[16,2,11,128]{3,1,2,0:T(2,128)(2,1)}, u32[]{:S(2)}, u32[]{:S(2)}) async-start(bf16[16,2,11,128]{3,1,2,0:T(2,128)(2,1)} %copy.102), calls=%async_computation.5 | async-start | bytes 180224 | tf_op jit(solution)/shard_map/all_to_all | solution.py:256
  280.7 2.9 add_convert_fusion
  283.6 10.2 %all-to-all-done.5 = bf16[16,2,11,128]{3,1,2,0:T(2,128)(2,1)} async-done(((bf16[16,2,11,128]{3,1,2,0:T(2,128)(2,1)}), bf16[16,2,11,128]{3,1,2,0:T(2,128)(2,1)}, u32[]{:S(2)}, u32[]{:S(2)}) %all-to-all-start.5) | async-done | bytes 90144 | tf_op jit(solution)/shard_map/all_to_all | solution.py:256
  293.8 5.6 %all-to-all-start.6 = ((bf16[8,448,128]{2,1,0:T(8,128)(2,1)}), bf16[8,448,128]{2,1,0:T(8,128)(2,1)}, u32[]{:S(2)}, u32[]{:S(2)}) async-start(bf16[8,448,128]{2,1,0:T(8,128)(2,1)} %add_convert_fusion), calls=%async_computation.6 | async-start | bytes 1835008 | tf_op jit(solution)/shard_map/all_to_all | solution.py:256
  301.0 8.2 %all-to-all-done.6 = bf16[8,448,128]{2,1,0:T(8,128)(2,1)} async-done(((bf16[8,448,128]{2,1,0:T(8,128)(2,1)}), bf16[8,448,128]{2,1,0:T(8,128)(2,1)}, u32[]{:S(2)}, u32[]{:S(2)}) %all-to-all-start.6) | async-done | bytes 917536 | tf_op jit(solution)/shard_map/all_to_all | solution.py:256
  309.2 2.1 slice_bitcast_fusion
  (87 shorter events, 30.4 us)
Async XLA Ops:
  0.6 1.8 copy-start
  0.6 21.4 %copy-start.10 = (s32[16]{0:T(128)S(1)}, s32[16]{0:T(128)}, u32[]{:S(2)}) copy-start(s32[16]{0:T(128)} %param.11) | copy-start | bytes 196
  3.3 28.5 %all-to-all-start.1 = ((bf16[16,2,11,128]{3,1,2,0:T(2,128)(2,1)}), bf16[16,2,11,128]{3,1,2,0:T(2,128)(2,1)S(1)}, u32[]{:S(2)}, u32[]{:S(2)}) async-start(bf16[16,2,11,128]{3,1,2,0:T(2,128)(2,1)} %copy.84), calls=%async_computation.1 | async-start | bytes 180224 | tf_op jit(solution)/shard_map/all_to_all | solution.py:256
  20.1 3.3 %collective-permute-start.1 = (bf16[2,16,11,224]{3,0,2,1:T(2,128)(2,1)S(1)}, bf16[2,16,11,224]{3,0,2,1:T(2,128)(2,1)S(1)}, u32[]{:S(2)}, u32[]{:S(2)}) collective-permute-start(bf16[2,16,11,224]{3,0,2,1:T(2,128)(2,1)S(1)} %fusion.1), channel_id=1, source_target_pairs={{0,1},{1,0},{2,3},{3,2},{4,5},{5,4},{6,7},{7,6},{8,9},{9,8},{10,11... | collective-permute-start | bytes 473096 | tf_op jit(solution)/shard_map/ppermute | solution.py:252
  22.5 10.0 %copy-start.12 = (s32[16]{0:T(128)}, s32[16]{0:T(128)S(1)}, u32[]{:S(2)}) copy-start(s32[16]{0:T(128)S(1)} %get-tuple-element.10) | copy-start | bytes 196
  23.8 17.4 %copy-start.9 = (f32[16,2,8]{0,2,1:T(8,128)S(1)}, f32[16,2,8]{0,2,1:T(8,128)}, u32[]{:S(2)}) copy-start(f32[16,2,8]{0,2,1:T(8,128)} %param.10) | copy-start | bytes 3076
  31.8 0.6 copy-start.8
  32.5 24.5 %all-to-all-start.2 = ((bf16[16,11,448]{2,1,0:T(8,128)(2,1)}), bf16[16,11,448]{2,1,0:T(8,128)(2,1)S(1)}, u32[]{:S(2)}, u32[]{:S(2)}) async-start(bf16[16,11,448]{2,1,0:T(8,128)(2,1)} %bitcast.87), calls=%async_computation.2 | async-start | bytes 524288 | tf_op jit(solution)/shard_map/all_to_all | solution.py:256
  38.5 2.2 copy-start.13
  41.2 21.6 %copy-start.11 = (s32[16]{0:T(128)S(1)}, s32[16]{0:T(128)}, u32[]{:S(2)}) copy-start(s32[16]{0:T(128)} %fusion.6) | copy-start | bytes 196
  57.0 7.3 %copy-start.7 = (bf16[16,11,448]{2,1,0:T(8,128)(2,1)}, bf16[16,11,448]{2,1,0:T(8,128)(2,1)S(1)}, u32[]{:S(2)}) copy-start(bf16[16,11,448]{2,1,0:T(8,128)(2,1)S(1)} %all-to-all-done.2) | copy-start | bytes 473092
  57.0 15.6 %all-to-all-start = ((bf16[8,448,128]{2,1,0:T(8,128)(2,1)}), bf16[8,448,128]{2,1,0:T(8,128)(2,1)}, u32[]{:S(2)}, u32[]{:S(2)}) async-start(bf16[8,448,128]{2,1,0:T(8,128)(2,1)} %pad_maximum_fusion), calls=%async_computation | async-start | bytes 1835008 | tf_op jit(solution)/shard_map/all_to_all | solution.py:256
  72.6 58.8 %all-to-all-start.3 = ((bf16[16,11,448]{2,1,0:T(8,128)(2,1)}), bf16[16,11,448]{2,1,0:T(8,128)(2,1)S(1)}, u32[]{:S(2)}, u32[]{:S(2)}) async-start(bf16[16,11,448]{2,1,0:T(8,128)(2,1)} %broadcast_select_fusion.6), calls=%async_computation.3 | async-start | bytes 524288 | tf_op jit(solution)/shard_map/all_to_all | solution.py:256
  86.5 45.9 %collective-permute-start = (bf16[8,448,128]{2,1,0:T(8,128)(2,1)}, bf16[8,448,128]{2,1,0:T(8,128)(2,1)}, u32[]{:S(2)}, u32[]{:S(2)}) collective-permute-start(bf16[8,448,128]{2,1,0:T(8,128)(2,1)} %all-to-all-done), channel_id=1, source_target_pairs={{0,1},{1,0},{2,3},{3,2},{4,5},{5,4},{6,7},{7,6},{8,9},{9,8},{10,11... | collective-permute-start | bytes 2752520 | tf_op jit(solution)/shard_map/ppermute | solution.py:252
  131.4 0.7 copy-start.6
  134.0 1.1 copy-start.1
  245.3 1.3 copy-start.2
  248.4 16.3 %all-to-all-start.4 = ((bf16[16,16,11,128]{3,1,2,0:T(8,128)(2,1)}), bf16[16,16,11,128]{3,1,2,0:T(8,128)(2,1)}, u32[]{:S(2)}, u32[]{:S(2)}) async-start(bf16[16,16,11,128]{3,1,2,0:T(8,128)(2,1)} %bitcast.84), calls=%async_computation.4 | async-start | bytes 1441792 | tf_op jit(solution)/shard_map/all_to_all | solution.py:256
  254.8 2.2 copy-start.5
  256.2 0.8 copy-start.3
  256.2 2.0 copy-start.4
  258.3 22.5 %collective-permute-start.2 = (bf16[8,448,128]{2,1,0:T(8,128)(2,1)}, bf16[8,448,128]{2,1,0:T(8,128)(2,1)}, u32[]{:S(2)}, u32[]{:S(2)}) collective-permute-start(bf16[8,448,128]{2,1,0:T(8,128)(2,1)} %broadcast_select_fusion), channel_id=1, source_target_pairs={{0,1},{1,0},{2,3},{3,2},{4,5},{5,4},{6,7},{7,6},{8,9},{9,8},{10,11... | collective-permute-start | bytes 2752520 | tf_op jit(solution)/shard_map/ppermute | solution.py:252
  270.3 23.4 %all-to-all-start.5 = ((bf16[16,2,11,128]{3,1,2,0:T(2,128)(2,1)}), bf16[16,2,11,128]{3,1,2,0:T(2,128)(2,1)}, u32[]{:S(2)}, u32[]{:S(2)}) async-start(bf16[16,2,11,128]{3,1,2,0:T(2,128)(2,1)} %copy.102), calls=%async_computation.5 | async-start | bytes 180224 | tf_op jit(solution)/shard_map/all_to_all | solution.py:256
  293.8 15.4 %all-to-all-start.6 = ((bf16[8,448,128]{2,1,0:T(8,128)(2,1)}), bf16[8,448,128]{2,1,0:T(8,128)(2,1)}, u32[]{:S(2)}, u32[]{:S(2)}) async-start(bf16[8,448,128]{2,1,0:T(8,128)(2,1)} %add_convert_fusion), calls=%async_computation.6 | async-start | bytes 1835008 | tf_op jit(solution)/shard_map/all_to_all | solution.py:256
where the time goes:
time: 313 us; the launch traced here: 311 us
  Pallas kernels  110 us (35%)
  starting transfers between devices  64.7 us (21%)
  waiting for transfers between devices  51.4 us (16%)
  blocking collectives  40.7 us (13%)
  local copies, waits for them, and re-layouts  27.5 us (9%)
  other arithmetic  15 us (5%)
    pallas_call x1, Pallas kernels, ring(): pl.pallas_call(functools.partial(ring_kernel, n), out_shape=(jax.ShapeDty...  110 us
    all_to_all x7, starting transfers between devices, exchange(): return lax.all_to_all(a, axes, split_axis=0, concat_axis=0, tiled=True)  59 us
    all_to_all x7, waiting for transfers between devices, exchange(): return lax.all_to_all(a, axes, split_axis=0, concat_axis=0, tiled=True)  50.5 us
    all_gather x1, blocking collectives, local(): lax.all_gather(mine, PLANE).transpose(1, 0, 2, 3)  40.7 us
    unnamed x34, local copies, waits for them, and re-layouts  8.28 us
  transfers between devices with their start and end apart: 10, of which 7 were waited for; matrix products, arithmetic and copies ran while one was open for 10% of the time, Pallas kernels for 0%

commit v1 on v0

v1 whole, which is shorter than its diff:
```python
import functools

import jax
import jax.numpy as jnp
from jax import lax
from jax.experimental import pallas as pl
from jax.experimental.pallas import tpu as pltpu
from jax.sharding import Mesh, PartitionSpec as P

MESH = pl.DeviceIdType.MESH
EXPERT = ("y_lo", "x")
PLANE = 16
ROWS = 176
TILES = 11
COLS = 224
PIECES = ((0, 48), (48, 48), (96, 48), (144, 32))
PARTS = ((0, 256), (256, 256), (512, 256), (768, 128))
NT = (((1,), (1,)), ((), ()))
TN = (((0,), (0,)), ((), ()))
f32, bf16 = jnp.float32, jnp.bfloat16


def loop(lo, hi, body):
    def step(i, carry):
        body(i)
        return carry

    lax.fori_loop(lo, hi, step, 0)


def kernel(
    n, counts, router, w_gate, w_up, tokens, upstream,
    out_tokens, out_gate, out_up,
    ids, rv, raw, zrecv, tokbuf, upsend, uprecv, upfull, up1, up2, upmoved,
    merged, stage, contrib, inbox, spread, acc,
    term, tg_out, tg_in, tg_send, tg_fin, sib_out, sib_in, wg_out,
    local_sem, w_send, w_recv, s_send, s_recv, tz_send, tz_recv, tp_send, tp_recv,
    us_sem, u1_send, u1_recv, u2_send, u2_recv,
    rs_send, rs_recv, ag_send, ag_recv,
    gp_send, gp_recv, gz_send, gz_recv, x_send, x_recv, e_send, e_recv,
):
    z = lax.axis_index("dp")
    y_lo, x, y_hi = lax.axis_index("y_lo"), lax.axis_index("x"), lax.axis_index("y_hi")
    core = lax.axis_index("core")
    expert = y_lo * 4 + x
    place = expert * 2 + y_hi
    half = n // 2
    experts = raw.shape[1]
    right, left = lax.rem(z + 1, n), lax.rem(z + n - 1, n)
    towards = (right, left)

    def on_plane(q, c):
        return {"y_lo": q // 8, "x": lax.rem(q // 2, 4), "y_hi": lax.rem(q, 2), "core": c}

    def on_expert(e):
        return {"y_lo": e // 4, "x": lax.rem(e, 4)}

    sibling = {"core": 1 - core}

    def remote(src, dst, send, recv, where):
        return pltpu.make_async_remote_copy(
            src_ref=src, dst_ref=dst, send_sem=send, recv_sem=recv,
            device_id=where, device_id_type=MESH,
        )

    def ahead(way, d):
        return lax.rem(z + d, n) if way == 0 else lax.rem(z + n - d, n)

    def behind(way, d):
        return ahead(1 - way, d)

    barrier = pltpu.get_barrier_semaphore()

    def greet(where):
        pl.semaphore_signal(barrier, inc=1, device_id=where, device_id_type=MESH)

    greet(sibling)
    loop(1, n, lambda k: greet({"dp": lax.rem(z + k, n)}))

    def greet_chip(k):
        q = lax.rem(place + k, PLANE)
        greet(on_plane(q, 0))
        greet(on_plane(q, 1))

    loop(1, PLANE, greet_chip)
    pl.semaphore_wait(barrier, 1 + (n - 1) + 2 * (PLANE - 1))

    tile = lax.rem(place + TILES * core, PLANE)
    serves = tile < TILES

    def token_block(to):
        rows = pl.ds(pl.multiple_of(core * ROWS + tile * 16, 16), 16)
        return tokens.at[:, rows, pl.ds(pl.multiple_of(to * 128, 128), 128)]

    def token_copy(k):
        to = lax.rem(z + k, n)
        return remote(token_block(to), zrecv.at[z], tz_send.at[k], tz_recv.at[k], {"dp": to})

    own_tokens = pltpu.make_async_copy(token_block(z), zrecv.at[z], local_sem.at[2])

    @pl.when(serves)
    def _():
        loop(1, n, lambda k: token_copy(k).start())
        own_tokens.start()

    stored = (w_gate, w_up)

    def weight_copy(k, w):
        to = lax.rem(expert + k, experts)
        return remote(
            stored[w].at[to], raw.at[core, expert, w], w_send.at[k, w], w_recv.at[k, w], on_expert(to)
        )

    def own_weights(w):
        return pltpu.make_async_copy(stored[w].at[expert], raw.at[core, expert, w], local_sem.at[w])

    for w in (0, 1):
        own_weights(w).start()

    def send_weights(k):
        for w in (0, 1):
            weight_copy(k, w).start()

    loop(1, experts, send_weights)

    row = lax.broadcasted_iota(jnp.int32, (ROWS, 2 * ROWS), 0)
    col = lax.broadcasted_iota(jnp.int32, (ROWS, 2 * ROWS), 1)
    unit = lax.broadcasted_iota(jnp.int32, (COLS, 512), 0)
    lane = lax.broadcasted_iota(jnp.int32, (COLS, 512), 1)
    tail = unit >= 192
    spot = jnp.where(
        tail, unit + (192 + 32 * core), (unit >> 6) * 128 + (unit & 63) + 64 * core
    )
    put = ((lane == spot) | (tail & (lane == spot + 64))).astype(f32).astype(bf16)

    def upstream_rows(k, which):
        pick = (col == row + ROWS * which).astype(f32).astype(bf16)
        turned = lax.dot_general(pick, upstream[k], NT, preferred_element_type=f32)
        return jnp.dot(turned.astype(bf16), put, preferred_element_type=f32).astype(bf16)

    for k in (0, 1):
        upsend[k] = upstream_rows(k, 1 - core)
    up_swap = remote(upsend, uprecv, us_sem.at[0], us_sem.at[1], sibling)
    up_swap.start()

    def ranks(g, carry):
        empties, doubles = carry
        ids[0, g] = empties
        ids[1, g] = doubles
        held = counts[g]
        return (
            empties + jnp.where(held == 0, 1, 0),
            doubles + jnp.where(held == 2, 1, 0),
        )

    lax.fori_loop(0, n, ranks, (jnp.int32(0), jnp.int32(0)))

    def pair(d):
        partner, helper = jnp.int32(0), jnp.int32(0)
        for g in range(n):
            lends = (counts[d] == 0) & (counts[g] == 2) & (ids[0, d] == ids[1, g])
            partner = partner + jnp.where(lends, g, 0)
            helps = (counts[g] == 0) & (counts[d] == 2) & (ids[0, g] == ids[1, d])
            helper = helper + jnp.where(helps, g, 0)
        ids[2, d] = partner
        ids[3, d] = helper
        source = jnp.where(counts[d] == 0, 2 * partner + 1, 2 * d)
        for e in range(experts):
            rv[d, e] = router[source, e]

    loop(0, n, pair)

    for k in (0, 1):
        upfull[k] = upstream_rows(k, core)

    def tile_copy(k):
        to = lax.rem(place + k, PLANE)
        return remote(
            tokbuf.at[tile], tokbuf.at[tile], tp_send.at[k], tp_recv.at[tile], on_plane(to, core)
        )

    @pl.when(serves)
    def _():
        loop(1, n, lambda k: token_copy(k).wait_recv())
        own_tokens.wait()

        def choose(v):
            lent, own = zrecv[ids[2, v], 1], zrecv[v, 0]
            tokbuf[tile, v] = jnp.where(counts[v] == 0, lent, own)

        loop(0, n, choose)
        loop(1, PLANE, lambda k: tile_copy(k).start())

    up_swap.wait()
    for k in (0, 1):
        upfull[k] = (upfull[k].astype(f32) + uprecv[k].astype(f32)).astype(bf16)

    def keeper(i):
        return lax.rem(i + half * core, n)

    kept = lax.rem(z + half * core, n)
    keeps = kept < TILES

    def scatter_copy(i):
        rows = pl.ds(pl.multiple_of(i * 16, 16), 16)
        return remote(
            upfull.at[1, rows], up1.at[z], u1_send.at[i], u1_recv.at[z], {"dp": keeper(i)}
        )

    def scatter(i):
        @pl.when(keeper(i) != z)
        def _():
            scatter_copy(i).start()

        @pl.when(keeper(i) == z)
        def _():
            up1[z] = upfull[1, pl.ds(pl.multiple_of(i * 16, 16), 16)]

    loop(0, TILES, scatter)

    def pass_block(e, w):
        return remote(
            raw.at[core, e, w], raw.at[core, e, w], s_send.at[e, w], s_recv.at[e, w], sibling
        )

    for w in (0, 1):
        own_weights(w).wait()
        pass_block(expert, w).start()

    def pass_weights(k):
        e = lax.rem(expert + experts - k, experts)
        for w in (0, 1):
            remote(
                stored[w].at[0], raw.at[core, e, w], w_send.at[k, w], w_recv.at[k, w], sibling
            ).wait_recv()
            pass_block(e, w).start()

    loop(1, experts, pass_weights)

    def await_weights(e):
        for w in (0, 1):
            remote(
                raw.at[core, e, w], raw.at[1 - core, e, w], s_send.at[e, w], s_recv.at[e, w], sibling
            ).wait_recv()

    loop(0, experts, await_weights)

    def await_tile(t):
        @pl.when(t != tile)
        def _():
            remote(
                tokbuf.at[t], tokbuf.at[t], tp_send.at[0], tp_recv.at[t], sibling
            ).wait_recv()

    loop(0, TILES, await_tile)

    def merge(v):
        weights = [rv[v, e] for e in range(experts)]

        def block(s, w, src, dst):
            total = weights[0] * raw[s, 0, w, src].astype(f32)
            for e in range(1, experts):
                total = total + weights[e] * raw[s, e, w, src].astype(f32)
            merged[v, dst] = total.astype(bf16)

        def tiles(q):
            for s in (0, 1):
                for w in (0, 1):
                    block(
                        s,
                        w,
                        pl.ds(pl.multiple_of(q * 64, 64), 64),
                        pl.ds(pl.multiple_of(w * 512 + q * 128 + s * 64, 64), 64),
                    )

        loop(0, 3, tiles)
        for s in (0, 1):
            for w in (0, 1):
                block(s, w, pl.ds(192, 32), pl.ds(384 + w * 64 + s * 32, 32))

    def tok(v):
        return tokbuf[:, v].reshape(ROWS, 128)

    def partial(v):
        return lax.dot_general(tok(v), merged[v], NT, preferred_element_type=f32)

    def rs_copy(way, d, p, src):
        rows = pl.ds(*PIECES[p])
        return remote(
            src.at[rows], inbox.at[way, d - 1, rows],
            rs_send.at[way, d - 1, p], rs_recv.at[way, d - 1, p], {"dp": towards[way]},
        )

    def ag_copy(way, d, p, v):
        rows = pl.ds(*PIECES[p])
        return remote(
            spread.at[v, rows], spread.at[v, rows],
            ag_send.at[way, d - 1, p], ag_recv.at[way, d - 1, p], {"dp": towards[way]},
        )

    def start_pieces(d, way):
        longer = (0, 1) if way == 0 else (2, 3)
        return longer if d == half else tuple(p for p in range(4) if p not in longer)

    far = ahead(0, half)
    merge(far)
    stage[0] = partial(far).astype(bf16)
    for way in (0, 1):
        for p in start_pieces(half, way):
            rs_copy(way, half, p, stage.at[0]).start()
    for way in (0, 1):
        v = ahead(way, half - 1)
        merge(v)
        contrib[(half - 1) % 2, way] = partial(v)
        for p in start_pieces(half - 1, way):
            rows = pl.ds(*PIECES[p])
            stage[1, rows] = contrib[(half - 1) % 2, way, rows].astype(bf16)
            rs_copy(way, half - 1, p, stage.at[1]).start()

    def gather_copy(k):
        to = lax.rem(z + k, n)
        rows = pl.ds(pl.multiple_of(kept * 16, 16), 16)
        return remote(up2.at[to], upmoved.at[rows], u2_send.at[k], u2_recv.at[kept], {"dp": to})

    @pl.when(keeps)
    def _():
        def await_scatter(k):
            g = lax.rem(z + k, n)
            remote(
                up2.at[0], up1.at[g], u1_send.at[0], u1_recv.at[g], {"dp": right}
            ).wait_recv()

        loop(1, n, await_scatter)

        def lend(d):
            up2[d] = up1[ids[2, d]]

        loop(0, n, lend)
        loop(1, n, lambda k: gather_copy(k).start())
        upmoved[pl.ds(pl.multiple_of(kept * 16, 16), 16)] = up2[z]

    def pass_on(way, d, p):
        rows = pl.ds(*PIECES[p])
        rs_copy(way, d + 1, p, inbox.at[way, d]).wait_recv()
        total = inbox[way, d, rows].astype(f32) + contrib[lax.rem(d, 2), way, rows]
        inbox[way, d, rows] = total.astype(bf16)
        rs_copy(way, d, p, inbox.at[way, d]).start()

    def prepare(d, i):
        way, second = i // 2, i % 2
        v = ahead(way, d)
        if second:
            contrib[lax.rem(d, 2), way] = partial(v)
        else:
            merge(v)

    for i in range(4):
        if i < 2:
            pass_on(0, half - 1, start_pieces(half, 0)[i])
            pass_on(1, half - 1, start_pieces(half, 1)[i])
        prepare(half - 2, i)

    def rs_step(i):
        d = half - 2 - i
        for j, (up, down) in enumerate(((2, 0), (3, 1), (0, 2), (1, 3))):
            pass_on(0, d, up)
            pass_on(1, d, down)
            prepare(d - 1, j)

    loop(0, half - 2, rs_step)

    def await_gather(i):
        @pl.when(i != kept)
        def _():
            rows = pl.ds(pl.multiple_of(i * 16, 16), 16)
            remote(
                up2.at[0], upmoved.at[rows], u2_send.at[0], u2_recv.at[i], {"dp": right}
            ).wait_recv()

    loop(0, TILES, await_gather)

    def gate_part(gate, up, flowing):
        s = jax.nn.sigmoid(gate)
        return (flowing * up * s * (1.0 + gate * (1.0 - s))).astype(bf16)

    def up_part(gate, flowing):
        return (flowing * gate * jax.nn.sigmoid(gate)).astype(bf16)

    for p in range(4):
        rows = pl.ds(*PIECES[p])
        for way in (0, 1):
            rs_copy(way, 1, p, inbox.at[way, 0]).wait_recv()
        pre = inbox[0, 0, rows].astype(f32) + inbox[1, 0, rows].astype(f32) + contrib[0, 0, rows]
        flowing = jnp.where(counts[z] == 0, upmoved[rows], upfull[0, rows]).astype(f32)
        gate, mixed, up = pre[:, :384], pre[:, 384:512], pre[:, 512:]
        spread[z, rows, :384] = gate_part(gate, up, flowing[:, :384])
        spread[z, rows, 512:] = up_part(gate, flowing[:, :384])
        low = lax.broadcasted_iota(jnp.int32, mixed.shape, 1) < 64
        rolled = pltpu.roll(mixed, 64, 1)
        gate, up = jnp.where(low, mixed, rolled), jnp.where(low, rolled, mixed)
        spread[z, rows, 384:512] = jnp.where(
            low, gate_part(gate, up, flowing[:, 384:]), up_part(gate, flowing[:, 384:])
        )
        for way in (0, 1):
            ag_copy(way, 1, p, z).start()

    acc[...] = jnp.zeros_like(acc)

    wide = lax.broadcasted_iota(jnp.int32, (PLANE * 16, ROWS), 0)
    slim = lax.broadcasted_iota(jnp.int32, (PLANE * 16, ROWS), 1)
    spare = (wide & 15) < TILES
    widen = (spare & (slim == (wide >> 4) * TILES + (wide & 15))).astype(f32).astype(bf16)
    my_block = x * 4 + y_hi * 2 + core

    def back(owners, i, unit):
        rows, hidden = pl.ds(*PIECES[i]), pl.ds(*PARTS[i])
        terms = []
        for j, v in enumerate(owners):
            term[j, rows] = jnp.dot(
                spread[v, rows], merged[v], preferred_element_type=f32
            ).astype(bf16)
            terms.append(
                lax.dot_general(spread[v, :, hidden], tok(v), TN, preferred_element_type=f32)
            )
            if i == 3:
                blocks = jnp.dot(widen, term[j], preferred_element_type=f32).astype(bf16)
                tg_out[:, unit + j] = blocks.reshape(PLANE, 16, 128)
        for e in range(experts):
            total = acc[e, hidden]
            for v, t in zip(owners, terms):
                total = total + rv[v, e] * t
            acc[e, hidden] = total
        if i == 3:
            send_terms(unit, len(owners))

    def term_copy(k, units):
        where = {"y_lo": core, "x": k // 4, "y_hi": lax.rem(k // 2, 2), "core": lax.rem(k, 2)}
        return remote(
            tg_out.at[k, units], tg_in.at[place, units], gp_send.at[k], gp_recv.at[place], where
        )

    def send_terms(unit, count):
        units = pl.ds(unit, count)

        def send(k):
            here = (y_lo == core) & (k == my_block)

            @pl.when(here)
            def _():
                tg_in[place, units] = tg_out[k, units]

            @pl.when(jnp.logical_not(here))
            def _():
                term_copy(k, units).start()

        loop(0, PLANE, send)

    def receive(way, d, p):
        ag_copy(way, d, p, behind(way, d)).wait_recv()

    def forward(way, d, p):
        ag_copy(way, d + 1, p, behind(way, d)).start()

    def ag_step(d, owners, last, unit):
        for p in range(4):
            for way in (0, 1):
                receive(way, d, p)
                if not last or p in start_pieces(half, way):
                    forward(way, d, p)
            back(owners, p, unit)

    ag_step(1, (z,), False, 0)
    loop(
        2,
        half - 1,
        lambda d: ag_step(d, (behind(0, d - 1), behind(1, d - 1)), False, 2 * d - 3),
    )
    ag_step(half - 1, (behind(0, half - 2), behind(1, half - 2)), True, n - 5)
    for i in range(4):
        back((behind(0, half - 1), behind(1, half - 1)), i, n - 3)
    for way in (0, 1):
        for p in start_pieces(half, way):
            receive(way, half, p)
    for i in range(4):
        back((far,), i, n - 1)

    other = 1 - core

    def units_of(w, s):
        for q in range(3):
            yield q * 64, 64, pl.ds(pl.multiple_of(w * 512 + q * 128 + s * 64, 64), 64)
        yield 192, 32, pl.ds(pl.multiple_of(384 + w * 64 + s * 32, 32), 32)

    def cross_copy(e):
        return remote(sib_out.at[e], sib_in.at[e], x_send.at[e], x_recv.at[e], sibling)

    def cross(e):
        for w in (0, 1):
            for at, size, hidden in units_of(w, other):
                sib_out[e, w, at : at + size] = acc[e, hidden].astype(bf16)
        cross_copy(e).start()

    loop(0, experts, cross)

    outs = (out_gate, out_up)

    def home_copy(k, w):
        to = lax.rem(expert + k, experts)
        return remote(
            wg_out.at[to, w], outs[w].at[expert], e_send.at[k, w], e_recv.at[k, w], on_expert(to)
        )

    def own_home(w):
        return pltpu.make_async_copy(wg_out.at[expert, w], outs[w].at[expert], local_sem.at[w])

    def settle(k):
        e = lax.rem(expert + k, experts)
        cross_copy(e).wait_recv()
        for w in (0, 1):
            for at, size, hidden in units_of(w, core):
                total = acc[e, hidden] + sib_in[e, w, at : at + size].astype(f32)
                wg_out[e, w, at : at + size] = total.astype(bf16)

        @pl.when(k < experts)
        def _():
            for w in (0, 1):
                home_copy(k, w).start()

    loop(1, experts + 1, settle)
    for w in (0, 1):
        own_home(w).start()

    def await_terms(q):
        @pl.when(jnp.logical_not((y_lo == core) & (q == place)))
        def _():
            remote(
                tg_in.at[q], tg_in.at[q], gp_send.at[0], gp_recv.at[q], sibling
            ).wait_recv()

    loop(0, PLANE, await_terms)
    sums = tg_in[0].astype(f32)
    for q in range(1, PLANE):
        sums = sums + tg_in[q].astype(f32)
    term_sum = tg_out.at[0]

    def await_sent(k):
        @pl.when(jnp.logical_not((y_lo == core) & (k == my_block)))
        def _():
            remote(
                tg_out.at[k], tg_in.at[0], gp_send.at[k], gp_recv.at[0], sibling
            ).wait_send()

    loop(0, PLANE, await_sent)
    term_sum[...] = sums.astype(bf16)

    def unit_of(v):
        apart = lax.rem(v - z + n, n)
        near = jnp.where(apart < half, 2 * apart, 2 * (n - apart) - 1)
        return jnp.where(apart == half, n - 1, near)

    def slots(g):
        nothing = jnp.zeros((16, 128), bf16)
        first, second = term_sum[unit_of(g)], term_sum[unit_of(ids[3, g])]
        tg_send[g, 0] = jnp.where(counts[g] == 0, nothing, first)
        tg_send[g, 1] = jnp.where(counts[g] == 2, second, nothing)

    loop(0, n, slots)

    def slot_copy(k):
        to = lax.rem(z + k, n)
        return remote(tg_send.at[to], tg_fin.at[z], gz_send.at[k], gz_recv.at[k], {"dp": to})

    loop(1, n, lambda k: slot_copy(k).start())
    tg_fin[z] = tg_send[z]

    for way in (0, 1):
        for p in range(4):
            reach = half if p in start_pieces(half, way) else half - 1

            def sent(d, way=way, p=p):
                rs_copy(way, d, p, inbox.at[way, 0]).wait_send()
                ag_copy(way, d, p, 0).wait_send()

            loop(1, reach + 1, sent)

    @pl.when(serves)
    def _():
        loop(1, n, lambda k: token_copy(k).wait_send())
        loop(1, PLANE, lambda k: tile_copy(k).wait_send())

    def weights_sent(k):
        for w in (0, 1):
            weight_copy(k, w).wait_send()

    loop(1, experts, weights_sent)

    def passed(e):
        for w in (0, 1):
            pass_block(e, w).wait_send()
        cross_copy(e).wait_send()

    loop(0, experts, passed)

    def scattered(i):
        @pl.when(keeper(i) != z)
        def _():
            scatter_copy(i).wait_send()

    loop(0, TILES, scattered)

    @pl.when(keeps)
    def _():
        loop(1, n, lambda k: gather_copy(k).wait_send())

    def home(k):
        for w in (0, 1):
            home_copy(k, w).wait()

    loop(1, experts, home)
    for w in (0, 1):
        own_home(w).wait()
    loop(1, n, lambda k: slot_copy(k).wait())
    out_tokens[...] = tg_fin[...]


def local(tokens, upstream, router, counts, w_gate, w_up):
    n = lax.axis_size("dp")
    _, slots, seg_len, width = tokens.shape
    _, depth, blocks, cols = w_gate.shape
    experts = router.shape[2]
    half = n // 2
    hidden = 4 * cols
    vmem, smem, hbm = (
        pl.BlockSpec(memory_space=space) for space in (pltpu.VMEM, pltpu.SMEM, pl.ANY)
    )
    dma = pltpu.SemaphoreType.DMA
    home = jax.ShapeDtypeStruct((blocks, cols, depth), bf16)
    tg, gate_grad, up_grad = pl.pallas_call(
        functools.partial(kernel, n),
        out_shape=(jax.ShapeDtypeStruct((n, slots, 16, depth), bf16), home, home),
        in_specs=[smem, smem, hbm, hbm, hbm, vmem],
        out_specs=(vmem, hbm, hbm),
        scratch_shapes=[
            pltpu.SMEM((4, n), jnp.int32),
            pltpu.SMEM((n, experts), f32),
            pltpu.VMEM((2, experts, 2, cols, depth), bf16),
            pltpu.VMEM((n, slots, 16, depth), bf16),
            pltpu.VMEM((TILES, n, 16, depth), bf16),
            pltpu.VMEM((slots, ROWS, 512), bf16),
            pltpu.VMEM((slots, ROWS, 512), bf16),
            pltpu.VMEM((slots, ROWS, 512), bf16),
            pltpu.VMEM((n, 16, 512), bf16),
            pltpu.VMEM((n, 16, 512), bf16),
            pltpu.VMEM((ROWS, 512), bf16),
            pltpu.VMEM((n, hidden, depth), bf16),
            pltpu.VMEM((2, ROWS, hidden), bf16),
            pltpu.VMEM((2, 2, ROWS, hidden), f32),
            pltpu.VMEM((2, half, ROWS, hidden), bf16),
            pltpu.VMEM((n, ROWS, hidden), bf16),
            pltpu.VMEM((experts, hidden, depth), f32),
            pltpu.VMEM((2, ROWS, depth), bf16),
            pltpu.VMEM((PLANE, n, 16, depth), bf16),
            pltpu.VMEM((PLANE, n, 16, depth), bf16),
            pltpu.VMEM((n, slots, 16, depth), bf16),
            pltpu.VMEM((n, slots, 16, depth), bf16),
            pltpu.VMEM((experts, 2, cols, depth), bf16),
            pltpu.VMEM((experts, 2, cols, depth), bf16),
            pltpu.VMEM((experts, 2, cols, depth), bf16),
            dma((3,)),
            dma((experts, 2)), dma((experts, 2)),
            dma((experts, 2)), dma((experts, 2)),
            dma((n,)), dma((n,)),
            dma((PLANE,)), dma((PLANE,)),
            dma((2,)),
            dma((TILES,)), dma((n,)),
            dma((n,)), dma((PLANE,)),
            dma((2, half, 4)), dma((2, half, 4)),
            dma((2, half, 4)), dma((2, half, 4)),
            dma((PLANE,)), dma((PLANE,)),
            dma((n,)), dma((n,)),
            dma((experts,)), dma((experts,)),
            dma((experts, 2)), dma((experts, 2)),
        ],
        compiler_params=pltpu.CompilerParams(
            collective_id=0, has_side_effects=True, vmem_limit_bytes=56 * 2**20
        ),
    )(
        counts,
        router.reshape(n * slots, experts),
        w_gate[0].transpose(1, 2, 0),
        w_up[0].transpose(1, 2, 0),
        tokens[0],
        upstream[0].transpose(0, 2, 1),
    )
    tokens_grad = tg[:, :, : seg_len // 32].transpose(1, 2, 0, 3).reshape(1, slots, -1, width)
    return (tokens_grad, gate_grad.transpose(2, 0, 1)[None], up_grad.transpose(2, 0, 1)[None])


def solution(mesh):
    shape = (mesh.shape["dp"], 2, mesh.shape["expert"] // 2, mesh.shape["tensor"] // 2, 2)
    fine = Mesh(mesh.devices.reshape(shape), ("dp", "y_lo", "x", "y_hi", "core"))
    tensor = ("y_hi", "core")
    weights = P(EXPERT, "dp", None, tensor)
    in_specs = (
        P("dp", None, None, None),
        P("dp", None, None, EXPERT + tensor),
        P(),
        P(),
        weights,
        weights,
    )
    out_specs = (P("dp", None, EXPERT + tensor, None), weights, weights)
    return jax.shard_map(local, mesh=fine, in_specs=in_specs, out_specs=out_specs, check_vma=False)
```

time: 313 us -> 186 us (0.59)
  the two profiles are of different devices: /device:TPU:2 before, /device:TPU:1 now
where the time goes in v1:
time: 186 us; the launch traced here: 185 us
  Pallas kernels  178 us (96%)
  local copies, waits for them, and re-layouts  6.62 us (4%)
    pallas_call x1, Pallas kernels, local(): pl.pallas_call(functools.partial(kernel, n), out_shape=(jax.ShapeDtypeStr...  178 us
    unnamed x3, local copies, waits for them, and re-layouts  5.01 us

profile of v1, /device:TPU:1, one launch (start us, length us, event | category | flops | bytes accessed | tf_op | source)
XLA Modules:
  0.0 184.9 jit_solution(15480447846930679499)
XLA Ops:
  0.6 1.4 copy.10
  2.0 177.6 %shard_map.85 = (bf16[16,2,16,128]{3,2,1,0:T(8,128)(2,1)}, bf16[8,224,128]{2,1,0:T(8,128)(2,1)}, bf16[8,224,128]{2,1,0:T(8,128)(2,1)}) custom-call(s32[16]{0:T(128)} %counts.1, f32[32,8]{1,0:T(8,128)} %bitcast.29, bf16[8,224,128]{2,1,0:T(8,128)(2,1)} %bitcast.24, bf16[8,224,128]{2,1,0:T(8,128)(2,1)} %bitcast.25, bf16[2,352,2048]{2,1,0:T(8,128)(2,1)} %bitcast.23, ...), custom_call_target="tpu_custom_call" | custom-call | tf_op jit(solution)/shard_map/pallas_call | solution.py:638
  179.6 0.9 slice_bitcast_fusion
  180.6 0.7 reshape.13
  181.3 1.8 copy.14
  183.1 1.8 copy.15
  (1 shorter events, 0.0 us)

commit v2 on v1

--- a/solution.py
+++ b/solution.py
@@ -14,6 +14,7 @@
 TILES = 11
 COLS = 224
 PIECES = ((0, 48), (48, 48), (96, 48), (144, 32))
+BATCHES = ((0, 3), (3, 13))
 PARTS = ((0, 256), (256, 256), (512, 256), (768, 128))
 NT = (((1,), (1,)), ((), ()))
 TN = (((0,), (0,)), ((), ()))
@@ -32,7 +33,7 @@
     n, counts, router, w_gate, w_up, tokens, upstream,
     out_tokens, out_gate, out_up,
     ids, rv, raw, zrecv, tokbuf, upsend, uprecv, upfull, up1, up2, upmoved,
-    merged, stage, contrib, inbox, spread, acc,
+    merged, contrib, inbox, spread, acc,
     term, tg_out, tg_in, tg_send, tg_fin, sib_out, sib_in, wg_out,
     local_sem, w_send, w_recv, s_send, s_recv, tz_send, tz_recv, tp_send, tp_recv,
     us_sem, u1_send, u1_recv, u2_send, u2_recv,
@@ -164,19 +165,52 @@
             helper = helper + jnp.where(helps, g, 0)
         ids[2, d] = partner
         ids[3, d] = helper
-        source = jnp.where(counts[d] == 0, 2 * partner + 1, 2 * d)
+        slot = jnp.where(counts[d] == 0, 1, 0)
+        group = jnp.where(counts[d] == 0, partner, d)
         for e in range(experts):
-            rv[d, e] = router[source, e]
+            rv[d, e] = router[slot, e, group]
 
     loop(0, n, pair)
 
     for k in (0, 1):
         upfull[k] = upstream_rows(k, core)
 
-    def tile_copy(k):
+    up_swap.wait()
+    for k in (0, 1):
+        upfull[k] = (upfull[k].astype(f32) + uprecv[k].astype(f32)).astype(bf16)
+
+    def keeper(i):
+        return lax.rem(i + half * core, n)
+
+    kept = lax.rem(z + half * core, n)
+    keeps = kept < TILES
+
+    def scatter_copy(i):
+        rows = pl.ds(pl.multiple_of(i * 16, 16), 16)
+        return remote(
+            upfull.at[1, rows], up1.at[z], u1_send.at[i], u1_recv.at[z], {"dp": keeper(i)}
+        )
+
+    def scatter(i):
+        @pl.when(keeper(i) != z)
+        def _():
+            scatter_copy(i).start()
+
+        @pl.when(keeper(i) == z)
+        def _():
+            up1[z] = upfull[1, pl.ds(pl.multiple_of(i * 16, 16), 16)]
+
+    loop(0, TILES, scatter)
+
+    def order(v):
+        return lax.rem(v - z + half + 1 + n, n)
+
+    def tile_copy(k, b):
         to = lax.rem(place + k, PLANE)
+        some = pl.ds(*BATCHES[b])
         return remote(
-            tokbuf.at[tile], tokbuf.at[tile], tp_send.at[k], tp_recv.at[tile], on_plane(to, core)
+            tokbuf.at[tile, some], tokbuf.at[tile, some],
+            tp_send.at[b, k], tp_recv.at[b, tile], on_plane(to, core),
         )
 
     @pl.when(serves)
@@ -186,37 +220,11 @@
 
         def choose(v):
             lent, own = zrecv[ids[2, v], 1], zrecv[v, 0]
-            tokbuf[tile, v] = jnp.where(counts[v] == 0, lent, own)
+            tokbuf[tile, order(v)] = jnp.where(counts[v] == 0, lent, own)
 
         loop(0, n, choose)
-        loop(1, PLANE, lambda k: tile_copy(k).start())
-
-    up_swap.wait()
-    for k in (0, 1):
-        upfull[k] = (upfull[k].astype(f32) + uprecv[k].astype(f32)).astype(bf16)
-
-    def keeper(i):
-        return lax.rem(i + half * core, n)
-
-    kept = lax.rem(z + half * core, n)
-    keeps = kept < TILES
-
-    def scatter_copy(i):
-        rows = pl.ds(pl.multiple_of(i * 16, 16), 16)
-        return remote(
-            upfull.at[1, rows], up1.at[z], u1_send.at[i], u1_recv.at[z], {"dp": keeper(i)}
-        )
-
-    def scatter(i):
-        @pl.when(keeper(i) != z)
-        def _():
-            scatter_copy(i).start()
-
-        @pl.when(keeper(i) == z)
-        def _():
-            up1[z] = upfull[1, pl.ds(pl.multiple_of(i * 16, 16), 16)]
-
-    loop(0, TILES, scatter)
+        for b in (0, 1):
+            loop(1, PLANE, lambda k, b=b: tile_copy(k, b).start())
 
     def pass_block(e, w):
         return remote(
@@ -237,6 +245,28 @@
 
     loop(1, experts, pass_weights)
 
+    def gather_copy(k):
+        to = lax.rem(z + k, n)
+        rows = pl.ds(pl.multiple_of(kept * 16, 16), 16)
+        return remote(up2.at[to], upmoved.at[rows], u2_send.at[k], u2_recv.at[kept], {"dp": to})
+
+    @pl.when(keeps)
+    def _():
+        def await_scatter(k):
+            g = lax.rem(z + k, n)
+            remote(
+                up2.at[0], up1.at[g], u1_send.at[0], u1_recv.at[g], {"dp": right}
+            ).wait_recv()
+
+        loop(1, n, await_scatter)
+
+        def lend(d):
+            up2[d] = up1[ids[2, d]]
+
+        loop(0, n, lend)
+        loop(1, n, lambda k: gather_copy(k).start())
+        upmoved[pl.ds(pl.multiple_of(kept * 16, 16), 16)] = up2[z]
+
     def await_weights(e):
         for w in (0, 1):
             remote(
@@ -245,14 +275,19 @@
 
     loop(0, experts, await_weights)
 
-    def await_tile(t):
-        @pl.when(t != tile)
-        def _():
-            remote(
-                tokbuf.at[t], tokbuf.at[t], tp_send.at[0], tp_recv.at[t], sibling
-            ).wait_recv()
-
-    loop(0, TILES, await_tile)
+    def await_tiles(b):
+        some = pl.ds(*BATCHES[b])
+
+        def await_tile(t):
+            @pl.when(t != tile)
+            def _():
+                remote(
+                    tokbuf.at[t, some], tokbuf.at[t, some], tp_send.at[b, 0], tp_recv.at[b, t], sibling
+                ).wait_recv()
+
+        loop(0, TILES, await_tile)
+
+    await_tiles(0)
 
     def merge(v):
         weights = [rv[v, e] for e in range(experts)]
@@ -279,16 +314,16 @@
                 block(s, w, pl.ds(192, 32), pl.ds(384 + w * 64 + s * 32, 32))
 
     def tok(v):
-        return tokbuf[:, v].reshape(ROWS, 128)
+        return tokbuf[:, order(v)].reshape(ROWS, 128)
 
     def partial(v):
         return lax.dot_general(tok(v), merged[v], NT, preferred_element_type=f32)
 
-    def rs_copy(way, d, p, src):
+    def rs_copy(way, d, p):
         rows = pl.ds(*PIECES[p])
         return remote(
-            src.at[rows], inbox.at[way, d - 1, rows],
-            rs_send.at[way, d - 1, p], rs_recv.at[way, d - 1, p], {"dp": towards[way]},
+            inbox.at[way, d, rows], inbox.at[way, d - 1, rows],
+            rs_send.at[way, p], rs_recv.at[way, d - 1, p], {"dp": towards[way]},
         )
 
     def ag_copy(way, d, p, v):
@@ -304,47 +339,28 @@
 
     far = ahead(0, half)
     merge(far)
-    stage[0] = partial(far).astype(bf16)
+    first = partial(far).astype(bf16)
     for way in (0, 1):
         for p in start_pieces(half, way):
-            rs_copy(way, half, p, stage.at[0]).start()
+            at, size = PIECES[p]
+            inbox[way, half, at : at + size] = first[at : at + size]
+            rs_copy(way, half, p).start()
     for way in (0, 1):
         v = ahead(way, half - 1)
         merge(v)
         contrib[(half - 1) % 2, way] = partial(v)
         for p in start_pieces(half - 1, way):
             rows = pl.ds(*PIECES[p])
-            stage[1, rows] = contrib[(half - 1) % 2, way, rows].astype(bf16)
-            rs_copy(way, half - 1, p, stage.at[1]).start()
-
-    def gather_copy(k):
-        to = lax.rem(z + k, n)
-        rows = pl.ds(pl.multiple_of(kept * 16, 16), 16)
-        return remote(up2.at[to], upmoved.at[rows], u2_send.at[k], u2_recv.at[kept], {"dp": to})
-
-    @pl.when(keeps)
-    def _():
-        def await_scatter(k):
-            g = lax.rem(z + k, n)
-            remote(
-                up2.at[0], up1.at[g], u1_send.at[0], u1_recv.at[g], {"dp": right}
-            ).wait_recv()
-
-        loop(1, n, await_scatter)
-
-        def lend(d):
-            up2[d] = up1[ids[2, d]]
-
-        loop(0, n, lend)
-        loop(1, n, lambda k: gather_copy(k).start())
-        upmoved[pl.ds(pl.multiple_of(kept * 16, 16), 16)] = up2[z]
+            inbox[way, half - 1, rows] = contrib[(half - 1) % 2, way, rows].astype(bf16)
+            rs_copy(way, half - 1, p).start()
+    await_tiles(1)
 
     def pass_on(way, d, p):
         rows = pl.ds(*PIECES[p])
-        rs_copy(way, d + 1, p, inbox.at[way, d]).wait_recv()
+        rs_copy(way, d + 1, p).wait_recv()
         total = inbox[way, d, rows].astype(f32) + contrib[lax.rem(d, 2), way, rows]
         inbox[way, d, rows] = total.astype(bf16)
-        rs_copy(way, d, p, inbox.at[way, d]).start()
+        rs_copy(way, d, p).start()
 
     def prepare(d, i):
         way, second = i // 2, i % 2
@@ -389,7 +405,7 @@
     for p in range(4):
         rows = pl.ds(*PIECES[p])
         for way in (0, 1):
-            rs_copy(way, 1, p, inbox.at[way, 0]).wait_recv()
+            rs_copy(way, 1, p).wait_recv()
         pre = inbox[0, 0, rows].astype(f32) + inbox[1, 0, rows].astype(f32) + contrib[0, 0, rows]
         flowing = jnp.where(counts[z] == 0, upmoved[rows], upfull[0, rows]).astype(f32)
         gate, mixed, up = pre[:, :384], pre[:, 384:512], pre[:, 512:]
@@ -578,15 +594,19 @@
             reach = half if p in start_pieces(half, way) else half - 1
 
             def sent(d, way=way, p=p):
-                rs_copy(way, d, p, inbox.at[way, 0]).wait_send()
                 ag_copy(way, d, p, 0).wait_send()
 
             loop(1, reach + 1, sent)
+            started = inbox.at[way, pl.ds(1, reach), pl.ds(*PIECES[p])]
+            remote(
+                started, started, rs_send.at[way, p], rs_recv.at[way, 0, p], sibling
+            ).wait_send()
 
     @pl.when(serves)
     def _():
         loop(1, n, lambda k: token_copy(k).wait_send())
-        loop(1, PLANE, lambda k: tile_copy(k).wait_send())
+        for b in (0, 1):
+            loop(1, PLANE, lambda k, b=b: tile_copy(k, b).wait_send())
 
     def weights_sent(k):
         for w in (0, 1):
@@ -621,6 +641,17 @@
         own_home(w).wait()
     loop(1, n, lambda k: slot_copy(k).wait())
     out_tokens[...] = tg_fin[...]
+
+
+def finish_kernel(gate, up, out_gate, out_up, sems):
+    pieces = sems.shape[1]
+    size = gate.shape[0] // pieces
+    for go in (True, False):
+        for w, (src, dst) in enumerate(((gate, out_gate), (up, out_up))):
+            for i in range(pieces):
+                some = pl.ds(i * size, size)
+                copy = pltpu.make_async_copy(src.at[some], dst.at[some], sems.at[w, i])
+                copy.start() if go else copy.wait()
 
 
 def local(tokens, upstream, router, counts, w_gate, w_up):
@@ -653,9 +684,8 @@
             pltpu.VMEM((n, 16, 512), bf16),
             pltpu.VMEM((ROWS, 512), bf16),
             pltpu.VMEM((n, hidden, depth), bf16),
-            pltpu.VMEM((2, ROWS, hidden), bf16),
             pltpu.VMEM((2, 2, ROWS, hidden), f32),
-            pltpu.VMEM((2, half, ROWS, hidden), bf16),
+            pltpu.VMEM((2, half + 1, ROWS, hidden), bf16),
             pltpu.VMEM((n, ROWS, hidden), bf16),
             pltpu.VMEM((experts, hidden, depth), f32),
             pltpu.VMEM((2, ROWS, depth), bf16),
@@ -670,11 +700,11 @@
             dma((experts, 2)), dma((experts, 2)),
             dma((experts, 2)), dma((experts, 2)),
             dma((n,)), dma((n,)),
-            dma((PLANE,)), dma((PLANE,)),
+            dma((2, PLANE)), dma((2, TILES)),
             dma((2,)),
             dma((TILES,)), dma((n,)),
             dma((n,)), dma((PLANE,)),
-            dma((2, half, 4)), dma((2, half, 4)),
+            dma((2, 4)), dma((2, half, 4)),
             dma((2, half, 4)), dma((2, half, 4)),
             dma((PLANE,)), dma((PLANE,)),
             dma((n,)), dma((n,)),
@@ -686,12 +716,19 @@
         ),
     )(
         counts,
-        router.reshape(n * slots, experts),
+        router.transpose(1, 2, 0),
         w_gate[0].transpose(1, 2, 0),
         w_up[0].transpose(1, 2, 0),
         tokens[0],
         upstream[0].transpose(0, 2, 1),
     )
+    gate_grad, up_grad = pl.pallas_call(
+        finish_kernel,
+        out_shape=(home, home),
+        in_specs=[vmem, vmem],
+        out_specs=(hbm, hbm),
+        scratch_shapes=[dma((2, 4))],
+    )(gate_grad, up_grad)
     tokens_grad = tg[:, :, : seg_len // 32].transpose(1, 2, 0, 3).reshape(1, slots, -1, width)
     return (tokens_grad, gate_grad.transpose(2, 0, 1)[None], up_grad.transpose(2, 0, 1)[None])
 

time: 186 us -> 174 us (0.935)
  Pallas kernels: 178 us -> 172 us
  local copies, waits for them, and re-layouts: 6.62 us -> 1.62 us
    pallas_call x1, Pallas kernels: 178 us -> 170 us  [local(): pl.pallas_call(functools.partial(kernel, n), out_shape=(jax.ShapeDtypeStr...]
    unnamed x3 -> x0, local copies, waits for them, and re-layouts: 5.01 us -> none
    pallas_call x0 -> x1, Pallas kernels: none -> 2.13 us  [local(): pl.pallas_call(finish_kernel, out_shape=(home, home), in_specs=[vmem, vme...]
where the time goes in v2:
time: 174 us
  Pallas kernels  172 us (99%)
    pallas_call x1, Pallas kernels, local(): pl.pallas_call(functools.partial(kernel, n), out_shape=(jax.ShapeDtypeStr...  170 us

profile of v2, /device:TPU:1, one launch (start us, length us, event | category | flops | bytes accessed | tf_op | source)
XLA Modules:
  0.0 174.0 jit_solution(4001642523338504572)
XLA Ops:
  0.6 169.6 %shard_map.85 = (bf16[16,2,16,128]{3,2,1,0:T(8,128)(2,1)}, bf16[8,224,128]{2,1,0:T(8,128)(2,1)}, bf16[8,224,128]{2,1,0:T(8,128)(2,1)}) custom-call(s32[16]{0:T(128)} %counts.1, f32[2,8,16]{2,1,0:T(8,128)} %bitcast.27, bf16[8,224,128]{2,1,0:T(8,128)(2,1)} %bitcast.24, bf16[8,224,128]{2,1,0:T(8,128)(2,1)} %bitcast.25, bf16[2,352,2048]{2,1,0:T(8,128)(2,1)} %bitcast.23, ...), custom_call_target="tpu_custom_call" | custom-call | tf_op jit(solution)/shard_map/pallas_call | solution.py:669
  170.3 0.9 slice_bitcast_fusion
  171.2 0.7 reshape.9
  171.9 2.1 %shard_map.86 = (bf16[8,224,128]{2,1,0:T(8,128)(2,1)}, bf16[8,224,128]{2,1,0:T(8,128)(2,1)}) custom-call(bf16[8,224,128]{2,1,0:T(8,128)(2,1)} %get-tuple-element.9.gate, bf16[8,224,128]{2,1,0:T(8,128)(2,1)} %get-tuple-element.10.up), custom_call_target="tpu_custom_call" | custom-call | tf_op jit(solution)/shard_map/pallas_call | solution.py:725
  (1 shorter events, 0.0 us)

commit v3 on v2

--- a/solution.py
+++ b/solution.py
@@ -223,8 +223,7 @@
             tokbuf[tile, order(v)] = jnp.where(counts[v] == 0, lent, own)
 
         loop(0, n, choose)
-        for b in (0, 1):
-            loop(1, PLANE, lambda k, b=b: tile_copy(k, b).start())
+        loop(1, PLANE, lambda k: tile_copy(k, 0).start())
 
     def pass_block(e, w):
         return remote(
@@ -244,6 +243,11 @@
             pass_block(e, w).start()
 
     loop(1, experts, pass_weights)
+
+    @pl.when(serves)
+    def _():
+        loop(1, PLANE, lambda k: tile_copy(k, 1).start())
+
 
     def gather_copy(k):
         to = lax.rem(z + k, n)
@@ -494,6 +498,44 @@
     ag_step(half - 1, (behind(0, half - 2), behind(1, half - 2)), True, n - 5)
     for i in range(4):
         back((behind(0, half - 1), behind(1, half - 1)), i, n - 3)
+
+    for way in (0, 1):
+        for p in range(4):
+            reach = half if p in start_pieces(half, way) else half - 1
+            started = inbox.at[way, pl.ds(1, reach), pl.ds(*PIECES[p])]
+            remote(
+                started, started, rs_send.at[way, p], rs_recv.at[way, 0, p], sibling
+            ).wait_send()
+
+    @pl.when(serves)
+    def _():
+        loop(1, n, lambda k: token_copy(k).wait_send())
+        for b in (0, 1):
+            loop(1, PLANE, lambda k, b=b: tile_copy(k, b).wait_send())
+
+    def weights_sent(k):
+        for w in (0, 1):
+            weight_copy(k, w).wait_send()
+
+    loop(1, experts, weights_sent)
+
+    def passed(e):
+        for w in (0, 1):
+            pass_block(e, w).wait_send()
+
+    loop(0, experts, passed)
+
+    def scattered(i):
+        @pl.when(keeper(i) != z)
+        def _():
+            scatter_copy(i).wait_send()
+
+    loop(0, TILES, scattered)
+
+    @pl.when(keeps)
+    def _():
+        loop(1, n, lambda k: gather_copy(k).wait_send())
+
     for way in (0, 1):
         for p in start_pieces(half, way):
             receive(way, half, p)
@@ -516,7 +558,7 @@
                 sib_out[e, w, at : at + size] = acc[e, hidden].astype(bf16)
         cross_copy(e).start()
 
-    loop(0, experts, cross)
+    loop(1, experts + 1, lambda k: cross(lax.rem(expert + k, experts)))
 
     outs = (out_gate, out_up)
 
@@ -592,45 +634,8 @@
     for way in (0, 1):
         for p in range(4):
             reach = half if p in start_pieces(half, way) else half - 1
-
-            def sent(d, way=way, p=p):
-                ag_copy(way, d, p, 0).wait_send()
-
-            loop(1, reach + 1, sent)
-            started = inbox.at[way, pl.ds(1, reach), pl.ds(*PIECES[p])]
-            remote(
-                started, started, rs_send.at[way, p], rs_recv.at[way, 0, p], sibling
-            ).wait_send()
-
-    @pl.when(serves)
-    def _():
-        loop(1, n, lambda k: token_copy(k).wait_send())
-        for b in (0, 1):
-            loop(1, PLANE, lambda k, b=b: tile_copy(k, b).wait_send())
-
-    def weights_sent(k):
-        for w in (0, 1):
-            weight_copy(k, w).wait_send()
-
-    loop(1, experts, weights_sent)
-
-    def passed(e):
-        for w in (0, 1):
-            pass_block(e, w).wait_send()
-        cross_copy(e).wait_send()
-
-    loop(0, experts, passed)
-
-    def scattered(i):
-        @pl.when(keeper(i) != z)
-        def _():
-            scatter_copy(i).wait_send()
-
-    loop(0, TILES, scattered)
-
-    @pl.when(keeps)
-    def _():
-        loop(1, n, lambda k: gather_copy(k).wait_send())
+            loop(1, reach + 1, lambda d, way=way, p=p: ag_copy(way, d, p, 0).wait_send())
+    loop(0, experts, lambda e: cross_copy(e).wait_send())
 
     def home(k):
         for w in (0, 1):

time: 174 us -> 174 us (level)
  no operation moved by 1% of the time
where the time goes in v3:
time: 174 us
  Pallas kernels  172 us (99%)
    pallas_call x1, Pallas kernels, local(): pl.pallas_call(functools.partial(kernel, n), out_shape=(jax.ShapeDtypeStr...  169 us

profile of v3, /device:TPU:1, one launch (start us, length us, event | category | flops | bytes accessed | tf_op | source)
XLA Modules:
  0.0 173.9 jit_solution(11968981954865485294)
XLA Ops:
  0.6 169.5 %shard_map.85 = (bf16[16,2,16,128]{3,2,1,0:T(8,128)(2,1)}, bf16[8,224,128]{2,1,0:T(8,128)(2,1)}, bf16[8,224,128]{2,1,0:T(8,128)(2,1)}) custom-call(s32[16]{0:T(128)} %counts.1, f32[2,8,16]{2,1,0:T(8,128)} %bitcast.27, bf16[8,224,128]{2,1,0:T(8,128)(2,1)} %bitcast.24, bf16[8,224,128]{2,1,0:T(8,128)(2,1)} %bitcast.25, bf16[2,352,2048]{2,1,0:T(8,128)(2,1)} %bitcast.23, ...), custom_call_target="tpu_custom_call" | custom-call | tf_op jit(solution)/shard_map/pallas_call | solution.py:674
  170.1 0.9 slice_bitcast_fusion
  171.1 0.7 reshape.9
  171.7 2.1 %shard_map.86 = (bf16[8,224,128]{2,1,0:T(8,128)(2,1)}, bf16[8,224,128]{2,1,0:T(8,128)(2,1)}) custom-call(bf16[8,224,128]{2,1,0:T(8,128)(2,1)} %get-tuple-element.9.gate, bf16[8,224,128]{2,1,0:T(8,128)(2,1)} %get-tuple-element.10.up), custom_call_target="tpu_custom_call" | custom-call | tf_op jit(solution)/shard_map/pallas_call | solution.py:730
  (1 shorter events, 0.0 us)

commit v4 on v3

--- a/solution.py
+++ b/solution.py
@@ -244,32 +244,6 @@
 
     loop(1, experts, pass_weights)
 
-    @pl.when(serves)
-    def _():
-        loop(1, PLANE, lambda k: tile_copy(k, 1).start())
-
-
-    def gather_copy(k):
-        to = lax.rem(z + k, n)
-        rows = pl.ds(pl.multiple_of(kept * 16, 16), 16)
-        return remote(up2.at[to], upmoved.at[rows], u2_send.at[k], u2_recv.at[kept], {"dp": to})
-
-    @pl.when(keeps)
-    def _():
-        def await_scatter(k):
-            g = lax.rem(z + k, n)
-            remote(
-                up2.at[0], up1.at[g], u1_send.at[0], u1_recv.at[g], {"dp": right}
-            ).wait_recv()
-
-        loop(1, n, await_scatter)
-
-        def lend(d):
-            up2[d] = up1[ids[2, d]]
-
-        loop(0, n, lend)
-        loop(1, n, lambda k: gather_copy(k).start())
-        upmoved[pl.ds(pl.multiple_of(kept * 16, 16), 16)] = up2[z]
 
     def await_weights(e):
         for w in (0, 1):
@@ -349,6 +323,11 @@
             at, size = PIECES[p]
             inbox[way, half, at : at + size] = first[at : at + size]
             rs_copy(way, half, p).start()
+
+    @pl.when(serves)
+    def _():
+        loop(1, PLANE, lambda k: tile_copy(k, 1).start())
+
     for way in (0, 1):
         v = ahead(way, half - 1)
         merge(v)
@@ -357,6 +336,28 @@
             rows = pl.ds(*PIECES[p])
             inbox[way, half - 1, rows] = contrib[(half - 1) % 2, way, rows].astype(bf16)
             rs_copy(way, half - 1, p).start()
+    def gather_copy(k):
+        to = lax.rem(z + k, n)
+        rows = pl.ds(pl.multiple_of(kept * 16, 16), 16)
+        return remote(up2.at[to], upmoved.at[rows], u2_send.at[k], u2_recv.at[kept], {"dp": to})
+
+    @pl.when(keeps)
+    def _():
+        def await_scatter(k):
+            g = lax.rem(z + k, n)
+            remote(
+                up2.at[0], up1.at[g], u1_send.at[0], u1_recv.at[g], {"dp": right}
+            ).wait_recv()
+
+        loop(1, n, await_scatter)
+
+        def lend(d):
+            up2[d] = up1[ids[2, d]]
+
+        loop(0, n, lend)
+        loop(1, n, lambda k: gather_copy(k).start())
+        upmoved[pl.ds(pl.multiple_of(kept * 16, 16), 16)] = up2[z]
+
     await_tiles(1)
 
     def pass_on(way, d, p):
@@ -433,25 +434,32 @@
     my_block = x * 4 + y_hi * 2 + core
 
     def back(owners, i, unit):
-        rows, hidden = pl.ds(*PIECES[i]), pl.ds(*PARTS[i])
-        terms = []
+        back_tokens(owners, i, unit)
+        back_weights(owners, i)
+        if i == 3:
+            send_terms(unit, len(owners))
+
+    def back_tokens(owners, i, unit):
+        rows = pl.ds(*PIECES[i])
         for j, v in enumerate(owners):
             term[j, rows] = jnp.dot(
                 spread[v, rows], merged[v], preferred_element_type=f32
             ).astype(bf16)
-            terms.append(
-                lax.dot_general(spread[v, :, hidden], tok(v), TN, preferred_element_type=f32)
-            )
             if i == 3:
                 blocks = jnp.dot(widen, term[j], preferred_element_type=f32).astype(bf16)
                 tg_out[:, unit + j] = blocks.reshape(PLANE, 16, 128)
+
+    def back_weights(owners, i):
+        hidden = pl.ds(*PARTS[i])
+        terms = [
+            lax.dot_general(spread[v, :, hidden], tok(v), TN, preferred_element_type=f32)
+            for v in owners
+        ]
         for e in range(experts):
             total = acc[e, hidden]
             for v, t in zip(owners, terms):
                 total = total + rv[v, e] * t
             acc[e, hidden] = total
-        if i == 3:
-            send_terms(unit, len(owners))
 
     def term_copy(k, units):
         where = {"y_lo": core, "x": k // 4, "y_hi": lax.rem(k // 2, 2), "core": lax.rem(k, 2)}
@@ -540,7 +548,7 @@
         for p in start_pieces(half, way):
             receive(way, half, p)
     for i in range(4):
-        back((far,), i, n - 1)
+        back_weights((far,), i)
 
     other = 1 - core
 
@@ -559,6 +567,9 @@
         cross_copy(e).start()
 
     loop(1, experts + 1, lambda k: cross(lax.rem(expert + k, experts)))
+    for i in range(4):
+        back_tokens((far,), i, n - 1)
+    send_terms(n - 1, 1)
 
     outs = (out_gate, out_up)
 

time: 174 us -> 175 us (level)
  no operation moved by 1% of the time
where the time goes in v4:
time: 175 us
  Pallas kernels  172 us (98%)
    pallas_call x1, Pallas kernels, local(): pl.pallas_call(functools.partial(kernel, n), out_shape=(jax.ShapeDtypeStr...  170 us

profile of v4, /device:TPU:1, one launch (start us, length us, event | category | flops | bytes accessed | tf_op | source)
XLA Modules:
  0.0 174.8 jit_solution(384754341245137168)
XLA Ops:
  0.6 170.4 %shard_map.85 = (bf16[16,2,16,128]{3,2,1,0:T(8,128)(2,1)}, bf16[8,224,128]{2,1,0:T(8,128)(2,1)}, bf16[8,224,128]{2,1,0:T(8,128)(2,1)}) custom-call(s32[16]{0:T(128)} %counts.1, f32[2,8,16]{2,1,0:T(8,128)} %bitcast.27, bf16[8,224,128]{2,1,0:T(8,128)(2,1)} %bitcast.24, bf16[8,224,128]{2,1,0:T(8,128)(2,1)} %bitcast.25, bf16[2,352,2048]{2,1,0:T(8,128)(2,1)} %bitcast.23, ...), custom_call_target="tpu_custom_call" | custom-call | tf_op jit(solution)/shard_map/pallas_call | solution.py:685
  171.0 0.9 slice_bitcast_fusion
  172.0 0.7 reshape.9
  172.6 2.1 %shard_map.86 = (bf16[8,224,128]{2,1,0:T(8,128)(2,1)}, bf16[8,224,128]{2,1,0:T(8,128)(2,1)}) custom-call(bf16[8,224,128]{2,1,0:T(8,128)(2,1)} %get-tuple-element.9.gate, bf16[8,224,128]{2,1,0:T(8,128)(2,1)} %get-tuple-element.10.up), custom_call_target="tpu_custom_call" | custom-call | tf_op jit(solution)/shard_map/pallas_call | solution.py:741
  (1 shorter events, 0.0 us)

commit v5 on v3

--- a/solution.py
+++ b/solution.py
@@ -244,10 +244,6 @@
 
     loop(1, experts, pass_weights)
 
-    @pl.when(serves)
-    def _():
-        loop(1, PLANE, lambda k: tile_copy(k, 1).start())
-
 
     def gather_copy(k):
         to = lax.rem(z + k, n)
@@ -349,6 +345,11 @@
             at, size = PIECES[p]
             inbox[way, half, at : at + size] = first[at : at + size]
             rs_copy(way, half, p).start()
+
+    @pl.when(serves)
+    def _():
+        loop(1, PLANE, lambda k: tile_copy(k, 1).start())
+
     for way in (0, 1):
         v = ahead(way, half - 1)
         merge(v)
@@ -433,25 +434,32 @@
     my_block = x * 4 + y_hi * 2 + core
 
     def back(owners, i, unit):
-        rows, hidden = pl.ds(*PIECES[i]), pl.ds(*PARTS[i])
-        terms = []
+        back_tokens(owners, i, unit)
+        back_weights(owners, i)
+        if i == 3:
+            send_terms(unit, len(owners))
+
+    def back_tokens(owners, i, unit):
+        rows = pl.ds(*PIECES[i])
         for j, v in enumerate(owners):
             term[j, rows] = jnp.dot(
                 spread[v, rows], merged[v], preferred_element_type=f32
             ).astype(bf16)
-            terms.append(
-                lax.dot_general(spread[v, :, hidden], tok(v), TN, preferred_element_type=f32)
-            )
             if i == 3:
                 blocks = jnp.dot(widen, term[j], preferred_element_type=f32).astype(bf16)
                 tg_out[:, unit + j] = blocks.reshape(PLANE, 16, 128)
+
+    def back_weights(owners, i):
+        hidden = pl.ds(*PARTS[i])
+        terms = [
+            lax.dot_general(spread[v, :, hidden], tok(v), TN, preferred_element_type=f32)
+            for v in owners
+        ]
         for e in range(experts):
             total = acc[e, hidden]
             for v, t in zip(owners, terms):
                 total = total + rv[v, e] * t
             acc[e, hidden] = total
-        if i == 3:
-            send_terms(unit, len(owners))
 
     def term_copy(k, units):
         where = {"y_lo": core, "x": k // 4, "y_hi": lax.rem(k // 2, 2), "core": lax.rem(k, 2)}
@@ -540,7 +548,7 @@
         for p in start_pieces(half, way):
             receive(way, half, p)
     for i in range(4):
-        back((far,), i, n - 1)
+        back_weights((far,), i)
 
     other = 1 - core
 
@@ -559,6 +567,9 @@
         cross_copy(e).start()
 
     loop(1, experts + 1, lambda k: cross(lax.rem(expert + k, experts)))
+    for i in range(4):
+        back_tokens((far,), i, n - 1)
+    send_terms(n - 1, 1)
 
     outs = (out_gate, out_up)
 

time: 174 us -> 175 us (level)
  no operation moved by 1% of the time
where the time goes in v5:
time: 175 us
  Pallas kernels  173 us (99%)
    pallas_call x1, Pallas kernels, local(): pl.pallas_call(functools.partial(kernel, n), out_shape=(jax.ShapeDtypeStr...  171 us

profile of v5, /device:TPU:1, one launch (start us, length us, event | category | flops | bytes accessed | tf_op | source)
XLA Modules:
  0.0 175.0 jit_solution(8960372150189750460)
XLA Ops:
  0.6 170.6 %shard_map.85 = (bf16[16,2,16,128]{3,2,1,0:T(8,128)(2,1)}, bf16[8,224,128]{2,1,0:T(8,128)(2,1)}, bf16[8,224,128]{2,1,0:T(8,128)(2,1)}) custom-call(s32[16]{0:T(128)} %counts.1, f32[2,8,16]{2,1,0:T(8,128)} %bitcast.27, bf16[8,224,128]{2,1,0:T(8,128)(2,1)} %bitcast.24, bf16[8,224,128]{2,1,0:T(8,128)(2,1)} %bitcast.25, bf16[2,352,2048]{2,1,0:T(8,128)(2,1)} %bitcast.23, ...), custom_call_target="tpu_custom_call" | custom-call | tf_op jit(solution)/shard_map/pallas_call | solution.py:685
  171.2 0.9 slice_bitcast_fusion
  172.2 0.7 reshape.9
  172.9 2.1 %shard_map.86 = (bf16[8,224,128]{2,1,0:T(8,128)(2,1)}, bf16[8,224,128]{2,1,0:T(8,128)(2,1)}) custom-call(bf16[8,224,128]{2,1,0:T(8,128)(2,1)} %get-tuple-element.9.gate, bf16[8,224,128]{2,1,0:T(8,128)(2,1)} %get-tuple-element.10.up), custom_call_target="tpu_custom_call" | custom-call | tf_op jit(solution)/shard_map/pallas_call | solution.py:741
  (1 shorter events, 0.0 us)
